TPU v7x, 512 devices: a whole 4x4x16 slice. The times are simulated.
512 devices in a mesh: prow: 16 (over z), pcol: 32 (over x, y, core).
Axes of the slice: x: 4, y: 4, z: 16, core: 2. Of those that a mesh axis runs over, the one named last changes fastest.
Arguments:
- matrix: float32 [8192, 8192], P('prow', 'pcol'), may hold values from -6 to 6
- factored_panel: float32 [8192, 256], P('prow', 'pcol')
- pivots: int32 [256], replicated, may hold values from 0 to 8191, as said below
Outputs:
- updated: float32 [8192, 8192], P('prow', 'pcol')
Inputs may be any that keep to these rules, and one draw needn't show every extreme that they name: pivots[j] is j or larger for every j; 8191 appears among the entries.
All inputs are finite; a program needn't handle non-finite values.
Results may differ from a plain program's by a relative error of at most 0.000055.
Values sent between devices are 32-bit elements; how exact they have to be, the bound alone decides.
No kernel may reach another device: no remote copies, remote signals or barrier semaphores. Data moves between devices by JAX's collectives and lax.ppermute only.
A program may use at most 64 MiB of HBM per device.

v0:
```python
from functools import partial

import jax
import jax.numpy as jnp
from jax import lax
from jax.experimental import pallas as pl
from jax.experimental.pallas import tpu as pltpu
from jax.sharding import PartitionSpec as P

HIGHEST = lax.Precision.HIGHEST
ROUNDS = (40, 48)
EARLY = 4
MAIN = 4
VMEM = pl.BlockSpec(memory_space=pltpu.VMEM)
HBM = pl.BlockSpec(memory_space=pltpu.HBM)
SMEM = pl.BlockSpec(memory_space=pltpu.SMEM)


def dot(a, b):
    return jnp.dot(a, b, precision=HIGHEST, preferred_element_type=jnp.float32)


class Table:
    ROW, PARTNER, OWN, COUNT, PLACE = range(5)


def spread_kernel(panel_ref, send_ref):
    nb = send_ref.shape[2]
    piece = panel_ref[:, :nb]
    for d in range(send_ref.shape[0]):
        send_ref[d] = piece


def join_kernel(panel_ref, pieces_ref, out_ref):
    rows = panel_ref.shape[1]
    out_ref[:, :rows] = panel_ref[...]
    out_ref[:, rows:] = pieces_ref[EARLY % pieces_ref.shape[0]]


def pack_kernel(pivots_ref, matrix_hbm, *refs):
    *send_refs, level_ref, table_ref, order_ref, fill_ref, matrix_ref, sem = refs
    nb = pivots_ref.shape[0]
    rows = matrix_ref.shape[0]
    planes = fill_ref.shape[0] // len(send_refs)
    rooms = [send_ref.shape[0] // planes for send_ref in send_refs]
    me = lax.axis_index("prow")
    bits = rows.bit_length() - 1
    fetch_matrix = pltpu.make_async_copy(matrix_hbm, matrix_ref, sem)
    fetch_matrix.start()

    def start(j, _):
        target = pivots_ref[j]
        order_ref[target] = target
        order_ref[j] = j
        return 0

    lax.fori_loop(0, nb, start, 0, unroll=16)

    def first_place(plane, room):
        return ((plane + MAIN) & (planes - 1)) * room

    for d in range(planes):
        for n, room in enumerate(rooms):
            fill_ref[n * planes + d] = first_place(d, room)

    mine_from = first_place(me, rooms[0])

    def exchange(j, _):
        target = pivots_ref[j]
        first = order_ref[j]
        row = order_ref[target]
        order_ref[target] = first
        table_ref[Table.ROW * nb + j] = row
        owner = row >> bits
        for n in range(len(rooms)):
            place = fill_ref[n * planes + owner]
            fill_ref[n * planes + owner] = place + 1
            table_ref[(Table.PLACE + n) * nb + j] = place
            if n == 0:
                own = Table.OWN * nb - mine_from + place
        table_ref[jnp.where(owner == me, own, Table.COUNT * nb)] = j
        return 0

    lax.fori_loop(0, nb, exchange, 0, unroll=16)
    count = fill_ref[me] - mine_from
    table_ref[Table.COUNT * nb] = count
    most = 0
    for d in range(1, planes):
        most = jnp.maximum(most, fill_ref[d] - first_place(d, rooms[0]))

    most = fill_ref[0] - first_place(0, rooms[0]) + most
    level = len(rooms)
    for n in reversed(range(len(rooms))):
        level = jnp.where(most <= rooms[n], n, level)
    level_ref[0] = level

    @pl.when((me == 0) & (level == len(rooms)))
    def _():
        def meet(i, _):
            table_ref[Table.PARTNER * nb + i] = order_ref[table_ref[Table.ROW * nb + i]]
            return 0

        lax.fori_loop(0, nb, meet, 0, unroll=16)

    fetch_matrix.wait()

    def fill(n, send_ref, room):
        def give(k, _):
            slot = table_ref[Table.OWN * nb + k]
            row = table_ref[Table.ROW * nb + slot]
            table_ref[Table.PARTNER * nb + slot] = order_ref[row]
            mine = row & (rows - 1)
            send_ref[pl.ds(k, 1), :] = matrix_ref[pl.ds(mine, 1), :]
            return 0

        lax.fori_loop(0, count, give, 0)
        given = send_ref[:room, :]
        for d in range(1, planes):
            send_ref[d * room : (d + 1) * room, :] = given

        @pl.when(me == 0)
        def _():
            def hand(i, _):
                row = table_ref[Table.ROW * nb + i]
                away = row >= rows
                partner = jnp.where(away, order_ref[row], 0)
                put = 2 * first_place(row >> bits, room) + room - 1 - table_ref[(Table.PLACE + n) * nb + i]
                put = jnp.where(away, put, (MAIN + 1) * room - 1)
                send_ref[pl.ds(put, 1), :] = matrix_ref[pl.ds(partner, 1), :]
                return 0

            lax.fori_loop(0, nb, hand, 0, unroll=16)

    for n, send_ref in enumerate(send_refs):
        pl.when(level == n)(partial(fill, n, send_ref, rooms[n]))


def slot_kernel(table_ref, matrix_ref, send_ref):
    planes, slots, _ = send_ref.shape
    nb = planes * slots
    rows = matrix_ref.shape[0]
    me = lax.axis_index("prow")

    def place(d, _):
        for k in range(slots):
            i = d * slots + k
            mine = table_ref[Table.ROW * nb + i] - me * rows
            owned = (mine >= 0) & (mine < rows)
            take = jnp.where(owned, mine, jnp.where(me == 0, table_ref[Table.PARTNER * nb + i], 0))
            send_ref[d, k : k + 1, :] = matrix_ref[pl.ds(take, 1), :]
        return 0

    lax.fori_loop(0, planes, place, 0)


def sort_kernel(rows, table_ref, arrived_ref, send_ref):
    planes, slots, _ = arrived_ref.shape
    me = lax.axis_index("prow")
    for k in range(slots):
        owner = table_ref[me * slots + k] // rows
        send_ref[0, k : k + 1, :] = arrived_ref[owner, k : k + 1, :]
    send_ref[0, slots:, :] = arrived_ref[0]
    both = send_ref[0]
    for d in range(1, planes):
        send_ref[d] = both


def invert_upper(block):
    size = block.shape[0]
    row = lax.broadcasted_iota(jnp.int32, (size, size), 0)
    col = lax.broadcasted_iota(jnp.int32, (size, size), 1)
    inverse = None
    width = 1
    while width < size:
        pair = ((row ^ col) & ~(2 * width - 1)) == 0
        cross = jnp.where(pair & ((row & width) == 0) & ((col & width) != 0), block, 0.0)
        if inverse is None:
            inverse = jnp.where(row == col, 1.0, 0.0) - cross
        else:
            inverse = inverse - dot(dot(inverse, cross), inverse)
        width *= 2
    return inverse


def invert_kernel(gathered_ref, panel_ref, inverse_ref, lower_ref):
    rows, nb = panel_ref.shape
    half = nb // 2
    inverse_ref[:half] = invert_upper(gathered_ref[:half, rows : rows + half]).T
    inverse_ref[half:] = invert_upper(gathered_ref[half:, rows + half :]).T
    lower_ref[...] = gathered_ref[:half, rows + half :].T
    panel_ref[...] = gathered_ref[:, :rows].T


def update_kernel(level, table_ref, panel_ref, inverse_ref, lower_ref, arrived_ref, matrix_ref, out_ref, upper_ref):
    planes, slots, cols = upper_ref.shape
    nb = planes * slots
    rows = matrix_ref.shape[0]
    room = arrived_ref.shape[0] // planes
    half = nb // 2
    me = lax.axis_index("prow")

    def pick(d, _):
        for k in range(slots):
            place = d * room + k
            if level is not None:
                place = table_ref[(Table.PLACE + level) * nb + d * slots + k]
            upper_ref[d, k : k + 1, :] = arrived_ref[pl.ds(place, 1), :]
        return 0

    lax.fori_loop(0, planes, pick, 0)
    out_ref[...] = matrix_ref[...]

    def patch(n, _):
        slot = table_ref[Table.OWN * nb + n]
        if level is not None:
            place = MAIN * room + jnp.where(me == 0, 0, room - 1 - n)
        else:
            place = slot // slots * room + slots + slot % slots
        far = arrived_ref[pl.ds(place, 1), :]
        lands = jnp.where(me == 0, jnp.minimum(table_ref[Table.PARTNER * nb + slot], rows - 1), 0)
        near = matrix_ref[pl.ds(lands, 1), :]
        out_ref[pl.ds(table_ref[Table.ROW * nb + slot] - me * rows, 1), :] = jnp.where(me == 0, near, far)
        return 0

    lax.fori_loop(0, table_ref[Table.COUNT * nb], patch, 0)
    upper = upper_ref[...].reshape(nb, cols)
    top = dot(inverse_ref[:half], upper[:half])
    rest = upper[half:] - dot(lower_ref[...], top)
    upper = jnp.concatenate([top, dot(inverse_ref[half:], rest)], axis=0)
    out_ref[...] -= dot(panel_ref[...], upper)

    @pl.when(me == 0)
    def _():
        out_ref[:nb, :] = upper


def call(kernel, outs, in_specs, out_specs, scratch=()):
    return pl.pallas_call(
        kernel,
        out_shape=outs,
        in_specs=in_specs,
        out_specs=out_specs,
        scratch_shapes=list(scratch),
        compiler_params=pltpu.CompilerParams(vmem_limit_bytes=16 * 1024 * 1024),
    )


def exchange(value, place):
    planes = value.shape[0]
    order = [[(p - place) % planes for p in range(planes)]]
    return lax.all_to_all(value, "prow", 0, 0, axis_index_groups=order)


def local(matrix, factored_panel, pivots):
    rows, cols = matrix.shape
    nb = pivots.shape[0]
    planes = lax.axis_size("prow")
    slots = nb // planes
    width = factored_panel.shape[1]
    rooms = ROUNDS
    f32 = jnp.float32
    panel = factored_panel.T
    pieces = call(spread_kernel, jax.ShapeDtypeStruct((planes, width, nb), f32), [VMEM], VMEM)(panel)
    pieces = exchange(pieces, EARLY)
    *sends, level, table = call(
        pack_kernel,
        (
            *(jax.ShapeDtypeStruct((planes * room, cols), f32) for room in rooms),
            jax.ShapeDtypeStruct((1,), jnp.int32),
            jax.ShapeDtypeStruct((8 * nb,), jnp.int32),
        ),
        [SMEM, HBM],
        (*(VMEM for _ in rooms), SMEM, SMEM),
        [
            pltpu.SMEM((rows * planes,), jnp.int32),
            pltpu.SMEM((len(rooms) * planes,), jnp.int32),
            pltpu.VMEM((rows, cols), f32),
            pltpu.SemaphoreType.DMA,
        ],
    )(pivots, matrix)

    def finish(level, table, panel, pieces, arrived, matrix):
        pieces = call(join_kernel, jax.ShapeDtypeStruct((width, rows + nb), f32), [VMEM, VMEM], VMEM)(panel, pieces)
        gathered = lax.all_gather(pieces, "pcol", axis=0, tiled=True)
        by_rows = call(
            invert_kernel,
            (
                jax.ShapeDtypeStruct((rows, nb), f32),
                jax.ShapeDtypeStruct((nb, nb // 2), f32),
                jax.ShapeDtypeStruct((nb // 2, nb // 2), f32),
            ),
            [VMEM],
            (VMEM, VMEM, VMEM),
        )(gathered)
        return call(
            partial(update_kernel, level),
            jax.ShapeDtypeStruct((rows, cols), f32),
            [SMEM, VMEM, VMEM, VMEM, VMEM, VMEM],
            VMEM,
            [pltpu.VMEM((planes, slots, cols), f32)],
        )(table, *by_rows, arrived, matrix)

    def one_round(level, sends, table, panel, pieces, matrix):
        arrived = exchange(sends[level].reshape(planes, rooms[level], cols), MAIN)
        return finish(level, table, panel, pieces, arrived.reshape(planes * rooms[level], cols), matrix)

    def two_rounds(sends, table, panel, pieces, matrix):
        slot = jax.ShapeDtypeStruct((planes, slots, cols), f32)
        both = jax.ShapeDtypeStruct((planes, 2 * slots, cols), f32)
        arrived = exchange(call(slot_kernel, slot, [SMEM, VMEM], VMEM)(table, matrix), 0)
        send = call(partial(sort_kernel, rows), both, [SMEM, VMEM], VMEM)(table, arrived)
        arrived = exchange(send, 0)
        return finish(None, table, panel, pieces, arrived.reshape(2 * nb, cols), matrix)

    forms = [*(partial(one_round, level) for level in range(len(rooms))), two_rounds]
    return lax.switch(level[0], forms, sends, table, panel, pieces, matrix)


def solution(mesh):
    return jax.shard_map(
        local,
        mesh=mesh,
        in_specs=(P("prow", "pcol"), P("prow", "pcol"), P()),
        out_specs=P("prow", "pcol"),
        check_vma=False,
    )
```

profile of v0, /device:TPU:1, one launch (start us, length us, event | category | flops | bytes accessed | tf_op | source)
XLA Modules:
  0.0 71.2 jit_solution(7159601295134280813)
XLA Ops:
  0.0 1.4 %shard_map.41 = f32[16,8,256]{2,1,0:T(8,128)} custom-call(f32[8,512]{1,0:T(8,128)} %bitcast.10), custom_call_target="tpu_custom_call" | custom-call | tf_op jit(solution)/shard_map/pallas_call | solution.py:263
  1.4 0.0 copy-start
  1.4 0.0 copy-start.1
  1.4 16.1 %all-to-all-start.4 = ((f32[16,8,256]{2,1,0:T(8,128)}), f32[16,8,256]{2,1,0:T(8,128)S(1)}, u32[]{:S(2)}, u32[]{:S(2)}) async-start(f32[16,8,256]{2,1,0:T(8,128)} %shard_map.41), calls=%async_computation.4 | async-start | bytes 262144 | tf_op jit(solution)/shard_map/all_to_all | solution.py:251
  17.5 0.0 copy-done
  17.5 0.0 copy-start.3
  17.5 6.5 %shard_map.40 = (f32[640,256]{1,0:T(8,128)}, f32[768,256]{1,0:T(8,128)}, s32[1]{0:T(128)}, s32[2048]{0:T(1024)S(1)}) custom-call(s32[256]{0:T(256)S(1)} %copy-done, f32[512,256]{1,0:T(8,128)} %matrix_hbm.1), custom_call_target="tpu_custom_call" | custom-call | tf_op jit(solution)/shard_map/pallas_call | solution.py:265
  24.6 2.6 %all-to-all-done.4 = f32[16,8,256]{2,1,0:T(8,128)S(1)} async-done(((f32[16,8,256]{2,1,0:T(8,128)}), f32[16,8,256]{2,1,0:T(8,128)S(1)}, u32[]{:S(2)}, u32[]{:S(2)}) %all-to-all-start.4) | async-done | bytes 131104 | tf_op jit(solution)/shard_map/all_to_all | solution.py:251
  27.3 0.0 copy-done.1
  27.3 0.0 copy-done.3
  27.3 43.1 %conditional.1 = (f32[512,256]{1,0:T(8,128)S(1)}) conditional(s32[]{:T(128)} %bitcast.5, (f32[8,512]{1,0:T(8,128)S(1)}, f32[16,8,256]{2,1,0:T(8,128)S(1)}, f32[640,256]{1,0:T(8,128)}, s32[2048]{0:T(1024)S(1)}, f32[512,256]{1,0:T(8,128)S(1)}) %tuple.27, (f32[8,512]{1,0:T(8,128)S(1)}, f32[16,8,256]{2,1,0:T(8,128)S(1)}, ...), branch_computations={%region_0.0_spmd, %region_1.0_spmd, %region_2.0_spmd} | conditional | bytes 3170344 | solution.py:316
  27.3 8.1 %all-to-all-start = ((f32[16,40,256]{2,1,0:T(8,128)}), f32[16,40,256]{2,1,0:T(8,128)S(1)}, u32[]{:S(2)}, u32[]{:S(2)}) async-start(f32[16,40,256]{2,1,0:T(8,128)} %bitcast), calls=%async_computation | async-start | bytes 1310720 | tf_op jit(solution)/shard_map/cond/branch_0_fun/all_to_all | solution.py:251
  35.4 26.9 %all_gather.6.gathered_ref = f32[256,768]{1,0:T(8,128)S(1)} all-gather(f32[8,768]{1,0:T(8,128)S(1)} %branch_0_fun.3), channel_id=1, replica_groups=mesh['prow'=16,'pcol'=32] {'pcol'}, dimensions={0}, use_global_device_ids=true | all-gather | bytes 811008 | tf_op jit(solution)/shard_map/cond/branch_0_fun/all_gather | solution.py:284
  62.3 4.8 %branch_0_fun.4 = (f32[512,256]{1,0:T(8,128)S(1)}, f32[256,128]{1,0:T(8,128)S(1)}, f32[128,128]{1,0:T(8,128)S(1)}) custom-call(f32[256,768]{1,0:T(8,128)S(1)} %all_gather.6.gathered_ref), custom_call_target="tpu_custom_call" | custom-call | tf_op jit(solution)/shard_map/cond/branch_0_fun/pallas_call | solution.py:285
  67.1 0.0 all-to-all-done
  67.1 3.1 %branch_0_fun.5 = f32[512,256]{1,0:T(8,128)S(1)} custom-call(s32[2048]{0:T(1024)S(1)} %get-tuple-element.36.table_ref, f32[512,256]{1,0:T(8,128)S(1)} %get-tuple-element.40.panel_ref, f32[256,128]{1,0:T(8,128)S(1)} %get-tuple-element.41.inverse_ref, f32[128,128]{1,0:T(8,128)S(1)} %get-tuple-element.42.lower_ref, f32[640,256]{1,0:T(8,128)S(1)} %bitcast.8, ...), custom_call_target="tpu_custom_call" | custom-call | tf_op jit(solution)/shard_map/cond/branch_0_fun/pallas_call | solution.py:295
  70.4 0.0 copy-start.2
  70.4 0.8 %copy-done.2 = f32[512,256]{1,0:T(8,128)} copy-done((f32[512,256]{1,0:T(8,128)}, f32[512,256]{1,0:T(8,128)S(1)}, u32[]{:S(2)}) %copy-start.2) | copy-done | bytes 524312
  (1 shorter events, 0.0 us)
Async XLA Ops:
  1.4 16.1 %copy-start = (s32[256]{0:T(256)S(1)}, s32[256]{0:T(256)}, u32[]{:S(2)}) copy-start(s32[256]{0:T(256)} %pivots_ref.1) | copy-start | bytes 3076
  1.4 25.9 %copy-start.1 = (f32[512,256]{1,0:T(8,128)S(1)}, f32[512,256]{1,0:T(8,128)}, u32[]{:S(2)}) copy-start(f32[512,256]{1,0:T(8,128)} %matrix_hbm.1) | copy-start | bytes 1572868
  1.4 25.9 %all-to-all-start.4 = ((f32[16,8,256]{2,1,0:T(8,128)}), f32[16,8,256]{2,1,0:T(8,128)S(1)}, u32[]{:S(2)}, u32[]{:S(2)}) async-start(f32[16,8,256]{2,1,0:T(8,128)} %shard_map.41), calls=%async_computation.4 | async-start | bytes 262144 | tf_op jit(solution)/shard_map/all_to_all | solution.py:251
  17.5 9.8 %copy-start.3 = (f32[512,8]{0,1:T(8,128)S(1)}, f32[512,8]{0,1:T(8,128)}, u32[]{:S(2)}) copy-start(f32[512,8]{0,1:T(8,128)} %param.7) | copy-start | bytes 49156
  27.3 39.8 %all-to-all-start = ((f32[16,40,256]{2,1,0:T(8,128)}), f32[16,40,256]{2,1,0:T(8,128)S(1)}, u32[]{:S(2)}, u32[]{:S(2)}) async-start(f32[16,40,256]{2,1,0:T(8,128)} %bitcast), calls=%async_computation | async-start | bytes 1310720 | tf_op jit(solution)/shard_map/cond/branch_0_fun/all_to_all | solution.py:251
  70.4 0.8 %copy-start.2 = (f32[512,256]{1,0:T(8,128)}, f32[512,256]{1,0:T(8,128)S(1)}, u32[]{:S(2)}) copy-start(f32[512,256]{1,0:T(8,128)S(1)} %get-tuple-element.76) | copy-start | bytes 1572868
where the time goes:
time: 71.5 us; the launch traced here: 71.2 us
  blocking collectives  26.9 us (38%)
  starting transfers between devices  24.2 us (34%)
  Pallas kernels  15.7 us (22%)
  waiting for transfers between devices  2.65 us (4%)
  local copies, waits for them, and re-layouts  0.8 us (1%)
    all_gather x1, blocking collectives, finish(): gathered = lax.all_gather(pieces, 'pcol', axis=0, tiled=True)  26.9 us
    all_to_all x2, starting transfers between devices, exchange(): return lax.all_to_all(value, 'prow', 0, 0, axis_index_groups=order)  24.2 us
    pallas_call x1, Pallas kernels, local(): call(pack_kernel, (*(jax.ShapeDtypeStruct((planes * room, cols), f32) for...  6.5 us
    pallas_call x1, Pallas kernels, finish(): call(invert_kernel, (jax.ShapeDtypeStruct((rows, nb), f32), jax.ShapeDtyp...  4.79 us
    pallas_call x1, Pallas kernels, finish(): call(partial(update_kernel, level), jax.ShapeDtypeStruct((rows, cols), f3...  3.08 us
    all_to_all x2, waiting for transfers between devices, exchange(): return lax.all_to_all(value, 'prow', 0, 0, axis_index_groups=order)  2.65 us
  transfers between devices with their start and end apart: 2, of which 1 were waited for; matrix products, arithmetic and copies ran while one was open for 0% of the time, Pallas kernels for 16%

commit v1 on v0

--- a/solution.py
+++ b/solution.py
@@ -199,15 +199,12 @@
     half = nb // 2
     me = lax.axis_index("prow")
 
-    def pick(d, _):
+    for d in range(planes):
         for k in range(slots):
             place = d * room + k
             if level is not None:
                 place = table_ref[(Table.PLACE + level) * nb + d * slots + k]
             upper_ref[d, k : k + 1, :] = arrived_ref[pl.ds(place, 1), :]
-        return 0
-
-    lax.fori_loop(0, planes, pick, 0)
     out_ref[...] = matrix_ref[...]
 
     def patch(n, _):

time: 71.5 us -> 76.6 us (1.071)
  the two profiles are of different devices: /device:TPU:1 before, /device:TPU:2 now
where the time goes in v1:
time: 76.6 us; the launch traced here: 76.2 us
  blocking collectives  24.9 us (33%)
  starting transfers between devices  23.5 us (31%)
  Pallas kernels  15.8 us (21%)
  waiting for transfers between devices  10.2 us (13%)
  local copies, waits for them, and re-layouts  0.8 us (1%)
    all_gather x1, blocking collectives, finish(): gathered = lax.all_gather(pieces, 'pcol', axis=0, tiled=True)  24.9 us
    all_to_all x2, starting transfers between devices, exchange(): return lax.all_to_all(value, 'prow', 0, 0, axis_index_groups=order)  23.5 us
    all_to_all x2, waiting for transfers between devices, exchange(): return lax.all_to_all(value, 'prow', 0, 0, axis_index_groups=order)  10.2 us
    pallas_call x1, Pallas kernels, local(): call(pack_kernel, (*(jax.ShapeDtypeStruct((planes * room, cols), f32) for...  6.61 us
    pallas_call x1, Pallas kernels, finish(): call(invert_kernel, (jax.ShapeDtypeStruct((rows, nb), f32), jax.ShapeDtyp...  4.78 us
    pallas_call x1, Pallas kernels, finish(): call(partial(update_kernel, level), jax.ShapeDtypeStruct((rows, cols), f3...  3 us
  transfers between devices with their start and end apart: 2, of which 2 were waited for; matrix products, arithmetic and copies ran while one was open for 0% of the time, Pallas kernels for 15%

profile of v1, /device:TPU:2, one launch (start us, length us, event | category | flops | bytes accessed | tf_op | source)
XLA Modules:
  0.0 76.2 jit_solution(6852487020965781178)
XLA Ops:
  0.0 1.4 %shard_map.41 = f32[16,8,256]{2,1,0:T(8,128)} custom-call(f32[8,512]{1,0:T(8,128)} %bitcast.10), custom_call_target="tpu_custom_call" | custom-call | tf_op jit(solution)/shard_map/pallas_call | solution.py:260
  1.4 0.0 copy-start
  1.4 0.0 copy-start.1
  1.4 15.8 %all-to-all-start.4 = ((f32[16,8,256]{2,1,0:T(8,128)}), f32[16,8,256]{2,1,0:T(8,128)S(1)}, u32[]{:S(2)}, u32[]{:S(2)}) async-start(f32[16,8,256]{2,1,0:T(8,128)} %shard_map.41), calls=%async_computation.4 | async-start | bytes 262144 | tf_op jit(solution)/shard_map/all_to_all | solution.py:248
  17.2 0.0 copy-done
  17.2 0.0 copy-start.3
  17.2 6.6 %shard_map.40 = (f32[640,256]{1,0:T(8,128)}, f32[768,256]{1,0:T(8,128)}, s32[1]{0:T(128)}, s32[2048]{0:T(1024)S(1)}) custom-call(s32[256]{0:T(256)S(1)} %copy-done, f32[512,256]{1,0:T(8,128)} %matrix_hbm.1), custom_call_target="tpu_custom_call" | custom-call | tf_op jit(solution)/shard_map/pallas_call | solution.py:262
  24.5 3.6 %all-to-all-done.4 = f32[16,8,256]{2,1,0:T(8,128)S(1)} async-done(((f32[16,8,256]{2,1,0:T(8,128)}), f32[16,8,256]{2,1,0:T(8,128)S(1)}, u32[]{:S(2)}, u32[]{:S(2)}) %all-to-all-start.4) | async-done | bytes 131104 | tf_op jit(solution)/shard_map/all_to_all | solution.py:248
  28.1 0.0 copy-done.1
  28.1 0.0 copy-done.3
  28.1 47.4 %conditional.1 = (f32[512,256]{1,0:T(8,128)S(1)}) conditional(s32[]{:T(128)} %bitcast.5, (f32[8,512]{1,0:T(8,128)S(1)}, f32[16,8,256]{2,1,0:T(8,128)S(1)}, f32[640,256]{1,0:T(8,128)}, s32[2048]{0:T(1024)S(1)}, f32[512,256]{1,0:T(8,128)S(1)}) %tuple.27, (f32[8,512]{1,0:T(8,128)S(1)}, f32[16,8,256]{2,1,0:T(8,128)S(1)}, ...), branch_computations={%region_0.0_spmd, %region_1.0_spmd, %region_2.0_spmd} | conditional | bytes 3170344 | solution.py:313
  28.1 7.7 %all-to-all-start.1 = ((f32[16,48,256]{2,1,0:T(8,128)}), f32[16,48,256]{2,1,0:T(8,128)S(1)}, u32[]{:S(2)}, u32[]{:S(2)}) async-start(f32[16,48,256]{2,1,0:T(8,128)} %bitcast.2), calls=%async_computation.1 | async-start | bytes 1572864 | tf_op jit(solution)/shard_map/cond/branch_1_fun/all_to_all | solution.py:248
  35.7 24.9 %all_gather.7.gathered_ref = f32[256,768]{1,0:T(8,128)S(1)} all-gather(f32[8,768]{1,0:T(8,128)S(1)} %branch_1_fun.3), channel_id=1, replica_groups=mesh['prow'=16,'pcol'=32] {'pcol'}, dimensions={0}, use_global_device_ids=true | all-gather | bytes 811008 | tf_op jit(solution)/shard_map/cond/branch_1_fun/all_gather | solution.py:281
  60.6 4.8 %branch_1_fun.4 = (f32[512,256]{1,0:T(8,128)S(1)}, f32[256,128]{1,0:T(8,128)S(1)}, f32[128,128]{1,0:T(8,128)S(1)}) custom-call(f32[256,768]{1,0:T(8,128)S(1)} %all_gather.7.gathered_ref), custom_call_target="tpu_custom_call" | custom-call | tf_op jit(solution)/shard_map/cond/branch_1_fun/pallas_call | solution.py:282
  65.4 6.6 %all-to-all-done.1 = f32[16,48,256]{2,1,0:T(8,128)S(1)} async-done(((f32[16,48,256]{2,1,0:T(8,128)}), f32[16,48,256]{2,1,0:T(8,128)S(1)}, u32[]{:S(2)}, u32[]{:S(2)}) %all-to-all-start.1) | async-done | bytes 786464 | tf_op jit(solution)/shard_map/cond/branch_1_fun/all_to_all | solution.py:248
  72.0 3.0 %branch_1_fun.5 = f32[512,256]{1,0:T(8,128)S(1)} custom-call(s32[2048]{0:T(1024)S(1)} %get-tuple-element.45.table_ref, f32[512,256]{1,0:T(8,128)S(1)} %get-tuple-element.48.panel_ref, f32[256,128]{1,0:T(8,128)S(1)} %get-tuple-element.49.inverse_ref, f32[128,128]{1,0:T(8,128)S(1)} %get-tuple-element.50.lower_ref, f32[768,256]{1,0:T(8,128)S(1)} %bitcast.7, ...), custom_call_target="tpu_custom_call" | custom-call | tf_op jit(solution)/shard_map/cond/branch_1_fun/pallas_call | solution.py:292
  75.4 0.0 copy-start.2
  75.4 0.8 %copy-done.2 = f32[512,256]{1,0:T(8,128)} copy-done((f32[512,256]{1,0:T(8,128)}, f32[512,256]{1,0:T(8,128)S(1)}, u32[]{:S(2)}) %copy-start.2) | copy-done | bytes 524312
  (1 shorter events, 0.0 us)
Async XLA Ops:
  1.4 15.8 %copy-start = (s32[256]{0:T(256)S(1)}, s32[256]{0:T(256)}, u32[]{:S(2)}) copy-start(s32[256]{0:T(256)} %pivots_ref.1) | copy-start | bytes 3076
  1.4 26.7 %copy-start.1 = (f32[512,256]{1,0:T(8,128)S(1)}, f32[512,256]{1,0:T(8,128)}, u32[]{:S(2)}) copy-start(f32[512,256]{1,0:T(8,128)} %matrix_hbm.1) | copy-start | bytes 1572868
  1.4 26.7 %all-to-all-start.4 = ((f32[16,8,256]{2,1,0:T(8,128)}), f32[16,8,256]{2,1,0:T(8,128)S(1)}, u32[]{:S(2)}, u32[]{:S(2)}) async-start(f32[16,8,256]{2,1,0:T(8,128)} %shard_map.41), calls=%async_computation.4 | async-start | bytes 262144 | tf_op jit(solution)/shard_map/all_to_all | solution.py:248
  17.2 10.9 %copy-start.3 = (f32[512,8]{0,1:T(8,128)S(1)}, f32[512,8]{0,1:T(8,128)}, u32[]{:S(2)}) copy-start(f32[512,8]{0,1:T(8,128)} %param.7) | copy-start | bytes 49156
  28.1 44.0 %all-to-all-start.1 = ((f32[16,48,256]{2,1,0:T(8,128)}), f32[16,48,256]{2,1,0:T(8,128)S(1)}, u32[]{:S(2)}, u32[]{:S(2)}) async-start(f32[16,48,256]{2,1,0:T(8,128)} %bitcast.2), calls=%async_computation.1 | async-start | bytes 1572864 | tf_op jit(solution)/shard_map/cond/branch_1_fun/all_to_all | solution.py:248
  75.4 0.8 %copy-start.2 = (f32[512,256]{1,0:T(8,128)}, f32[512,256]{1,0:T(8,128)S(1)}, u32[]{:S(2)}) copy-start(f32[512,256]{1,0:T(8,128)S(1)} %get-tuple-element.76) | copy-start | bytes 1572868

commit v2 on v1

--- a/solution.py
+++ b/solution.py
@@ -169,16 +169,22 @@
     size = block.shape[0]
     row = lax.broadcasted_iota(jnp.int32, (size, size), 0)
     col = lax.broadcasted_iota(jnp.int32, (size, size), 1)
-    inverse = None
-    width = 1
+
+    def cross(width):
+        pair = ((row ^ col) & ~(2 * width - 1)) == 0
+        return jnp.where(pair & ((row & width) == 0) & ((col & width) != 0), block, 0.0)
+
+    inverse = jnp.where(row == col, 1.0, 0.0) - cross(1)
+    width = 2
     while width < size:
-        pair = ((row ^ col) & ~(2 * width - 1)) == 0
-        cross = jnp.where(pair & ((row & width) == 0) & ((col & width) != 0), block, 0.0)
-        if inverse is None:
-            inverse = jnp.where(row == col, 1.0, 0.0) - cross
-        else:
-            inverse = inverse - dot(dot(inverse, cross), inverse)
-        width *= 2
+        near = dot(inverse, cross(width))
+        if 2 * width < size:
+            far = dot(inverse, cross(2 * width))
+            far = far - dot(near, far)
+        inverse = inverse - dot(near, inverse)
+        if 2 * width < size:
+            inverse = inverse - dot(far, inverse)
+        width *= 4
     return inverse
 
 

time: 76.6 us -> 71.4 us (0.932)
  the two profiles are of different devices: /device:TPU:2 before, /device:TPU:1 now
where the time goes in v2:
time: 71.4 us; the launch traced here: 70.3 us
  blocking collectives  26.9 us (38%)
  starting transfers between devices  24.2 us (34%)
  Pallas kernels  14.8 us (21%)
  waiting for transfers between devices  2.7 us (4%)
  local copies, waits for them, and re-layouts  0.8 us (1%)
    all_gather x1, blocking collectives, finish(): gathered = lax.all_gather(pieces, 'pcol', axis=0, tiled=True)  26.9 us
    all_to_all x2, starting transfers between devices, exchange(): return lax.all_to_all(value, 'prow', 0, 0, axis_index_groups=order)  24.2 us
    pallas_call x1, Pallas kernels, local(): call(pack_kernel, (*(jax.ShapeDtypeStruct((planes * room, cols), f32) for...  6.44 us
    pallas_call x1, Pallas kernels, finish(): call(invert_kernel, (jax.ShapeDtypeStruct((rows, nb), f32), jax.ShapeDtyp...  4.11 us
    pallas_call x1, Pallas kernels, finish(): call(partial(update_kernel, level), jax.ShapeDtypeStruct((rows, cols), f3...  2.83 us
    all_to_all x2, waiting for transfers between devices, exchange(): return lax.all_to_all(value, 'prow', 0, 0, axis_index_groups=order)  2.7 us
  transfers between devices with their start and end apart: 2, of which 1 were waited for; matrix products, arithmetic and copies ran while one was open for 0% of the time, Pallas kernels for 15%

profile of v2, /device:TPU:1, one launch (start us, length us, event | category | flops | bytes accessed | tf_op | source)
XLA Modules:
  0.0 70.3 jit_solution(10327290058062700903)
XLA Ops:
  0.0 1.4 %shard_map.41 = f32[16,8,256]{2,1,0:T(8,128)} custom-call(f32[8,512]{1,0:T(8,128)} %bitcast.10), custom_call_target="tpu_custom_call" | custom-call | tf_op jit(solution)/shard_map/pallas_call | solution.py:266
  1.4 0.0 copy-start
  1.4 0.0 copy-start.1
  1.4 16.1 %all-to-all-start.4 = ((f32[16,8,256]{2,1,0:T(8,128)}), f32[16,8,256]{2,1,0:T(8,128)S(1)}, u32[]{:S(2)}, u32[]{:S(2)}) async-start(f32[16,8,256]{2,1,0:T(8,128)} %shard_map.41), calls=%async_computation.4 | async-start | bytes 262144 | tf_op jit(solution)/shard_map/all_to_all | solution.py:254
  17.5 0.0 copy-done
  17.5 0.0 copy-start.3
  17.5 6.4 %shard_map.40 = (f32[640,256]{1,0:T(8,128)}, f32[768,256]{1,0:T(8,128)}, s32[1]{0:T(128)}, s32[2048]{0:T(1024)S(1)}) custom-call(s32[256]{0:T(256)S(1)} %copy-done, f32[512,256]{1,0:T(8,128)} %matrix_hbm.1), custom_call_target="tpu_custom_call" | custom-call | tf_op jit(solution)/shard_map/pallas_call | solution.py:268
  24.6 2.7 %all-to-all-done.4 = f32[16,8,256]{2,1,0:T(8,128)S(1)} async-done(((f32[16,8,256]{2,1,0:T(8,128)}), f32[16,8,256]{2,1,0:T(8,128)S(1)}, u32[]{:S(2)}, u32[]{:S(2)}) %all-to-all-start.4) | async-done | bytes 131104 | tf_op jit(solution)/shard_map/all_to_all | solution.py:254
  27.3 0.0 copy-done.1
  27.3 0.0 copy-done.3
  27.3 42.2 %conditional.1 = (f32[512,256]{1,0:T(8,128)S(1)}) conditional(s32[]{:T(128)} %bitcast.5, (f32[8,512]{1,0:T(8,128)S(1)}, f32[16,8,256]{2,1,0:T(8,128)S(1)}, f32[640,256]{1,0:T(8,128)}, s32[2048]{0:T(1024)S(1)}, f32[512,256]{1,0:T(8,128)S(1)}) %tuple.27, (f32[8,512]{1,0:T(8,128)S(1)}, f32[16,8,256]{2,1,0:T(8,128)S(1)}, ...), branch_computations={%region_0.0_spmd, %region_1.0_spmd, %region_2.0_spmd} | conditional | bytes 3170344 | solution.py:319
  27.3 8.1 %all-to-all-start = ((f32[16,40,256]{2,1,0:T(8,128)}), f32[16,40,256]{2,1,0:T(8,128)S(1)}, u32[]{:S(2)}, u32[]{:S(2)}) async-start(f32[16,40,256]{2,1,0:T(8,128)} %bitcast), calls=%async_computation | async-start | bytes 1310720 | tf_op jit(solution)/shard_map/cond/branch_0_fun/all_to_all | solution.py:254
  35.4 26.9 %all_gather.6.gathered_ref = f32[256,768]{1,0:T(8,128)S(1)} all-gather(f32[8,768]{1,0:T(8,128)S(1)} %branch_0_fun.3), channel_id=1, replica_groups=mesh['prow'=16,'pcol'=32] {'pcol'}, dimensions={0}, use_global_device_ids=true | all-gather | bytes 811008 | tf_op jit(solution)/shard_map/cond/branch_0_fun/all_gather | solution.py:287
  62.3 4.1 %branch_0_fun.4 = (f32[512,256]{1,0:T(8,128)S(1)}, f32[256,128]{1,0:T(8,128)S(1)}, f32[128,128]{1,0:T(8,128)S(1)}) custom-call(f32[256,768]{1,0:T(8,128)S(1)} %all_gather.6.gathered_ref), custom_call_target="tpu_custom_call" | custom-call | tf_op jit(solution)/shard_map/cond/branch_0_fun/pallas_call | solution.py:288
  66.4 0.0 all-to-all-done
  66.4 2.8 %branch_0_fun.5 = f32[512,256]{1,0:T(8,128)S(1)} custom-call(s32[2048]{0:T(1024)S(1)} %get-tuple-element.36.table_ref, f32[512,256]{1,0:T(8,128)S(1)} %get-tuple-element.40.panel_ref, f32[256,128]{1,0:T(8,128)S(1)} %get-tuple-element.41.inverse_ref, f32[128,128]{1,0:T(8,128)S(1)} %get-tuple-element.42.lower_ref, f32[640,256]{1,0:T(8,128)S(1)} %bitcast.8, ...), custom_call_target="tpu_custom_call" | custom-call | tf_op jit(solution)/shard_map/cond/branch_0_fun/pallas_call | solution.py:298
  69.5 0.0 copy-start.2
  69.5 0.8 %copy-done.2 = f32[512,256]{1,0:T(8,128)} copy-done((f32[512,256]{1,0:T(8,128)}, f32[512,256]{1,0:T(8,128)S(1)}, u32[]{:S(2)}) %copy-start.2) | copy-done | bytes 524312
  (1 shorter events, 0.0 us)
Async XLA Ops:
  1.4 16.1 %copy-start = (s32[256]{0:T(256)S(1)}, s32[256]{0:T(256)}, u32[]{:S(2)}) copy-start(s32[256]{0:T(256)} %pivots_ref.1) | copy-start | bytes 3076
  1.4 25.9 %copy-start.1 = (f32[512,256]{1,0:T(8,128)S(1)}, f32[512,256]{1,0:T(8,128)}, u32[]{:S(2)}) copy-start(f32[512,256]{1,0:T(8,128)} %matrix_hbm.1) | copy-start | bytes 1572868
  1.4 25.9 %all-to-all-start.4 = ((f32[16,8,256]{2,1,0:T(8,128)}), f32[16,8,256]{2,1,0:T(8,128)S(1)}, u32[]{:S(2)}, u32[]{:S(2)}) async-start(f32[16,8,256]{2,1,0:T(8,128)} %shard_map.41), calls=%async_computation.4 | async-start | bytes 262144 | tf_op jit(solution)/shard_map/all_to_all | solution.py:254
  17.5 9.8 %copy-start.3 = (f32[512,8]{0,1:T(8,128)S(1)}, f32[512,8]{0,1:T(8,128)}, u32[]{:S(2)}) copy-start(f32[512,8]{0,1:T(8,128)} %param.7) | copy-start | bytes 49156
  27.3 39.1 %all-to-all-start = ((f32[16,40,256]{2,1,0:T(8,128)}), f32[16,40,256]{2,1,0:T(8,128)S(1)}, u32[]{:S(2)}, u32[]{:S(2)}) async-start(f32[16,40,256]{2,1,0:T(8,128)} %bitcast), calls=%async_computation | async-start | bytes 1310720 | tf_op jit(solution)/shard_map/cond/branch_0_fun/all_to_all | solution.py:254
  69.5 0.8 %copy-start.2 = (f32[512,256]{1,0:T(8,128)}, f32[512,256]{1,0:T(8,128)S(1)}, u32[]{:S(2)}) copy-start(f32[512,256]{1,0:T(8,128)S(1)} %get-tuple-element.76) | copy-start | bytes 1572868
